TPU v7x, 128 devices: a whole 4x4x4 slice. The times are simulated.
128 devices in a mesh: row: 32 (over z, y, core), grp: 4 (over x).
Axes of the slice: x: 4, y: 4, z: 4, core: 2. Of those that a mesh axis runs over, the one named last changes fastest.
Arguments:
- tiles: float32 [2048, 20, 128, 128], P(('row', 'grp')), may hold values from 0.01 to 1
- tile_cols: int32 [2048, 20], P(('row', 'grp')), may hold values from 0 to 2047, as said below
- tile_counts: int32 [2048], P(('row', 'grp')), may hold values from 8 to 20, as said below
- block: float32 [262144, 128], P(('row', 'grp')), may hold values from -6 to 6
Outputs:
- next_block: float32 [262144, 128], P(('row', 'grp'))
Inputs may be any that keep to these rules, and one draw needn't show every extreme that they name: `tile_counts`: every tile-row has at least 8 live tiles and every device has a tile-row with all 20 live. `tile_cols`: device p (in the order of row then grp) owns tile-columns p * 16 to (p + 1) * 16 - 1. For every ordered pair of different devices, exactly 1 live tiles of the first refer to tile-columns owned by the second; every other slot, live or not, refers to a tile-column of its own device.
All inputs are finite; a program needn't handle non-finite values.
Results may differ from a plain program's by a relative error of at most 0.0003.
Values sent between devices are 32-bit elements; how exact they have to be, the bound alone decides.
A program may use at most 192 MiB of HBM per device.

v0:
```python
import jax
import jax.numpy as jnp
from jax import lax
from jax.sharding import PartitionSpec as P

REMOTE = 1
ITERS = 2


def weighted_sum(tile_set, vectors, weights):
    return jnp.einsum(
        "sij,sjk,st->tik", tile_set, vectors, weights, precision=lax.Precision.HIGHEST
    )


def per_device(tiles, tile_cols, tile_counts, block):
    devices_all = lax.axis_size(("row", "grp"))
    own_index = lax.axis_index(("row", "grp"))
    tile_rows, slot_count, tile_size, _ = tiles.shape
    columns = block.shape[1]
    slot_total = tile_rows * slot_count
    live_mask = (jnp.arange(slot_count)[None, :] < tile_counts[:, None]).astype(jnp.float32)
    degree = jnp.einsum("rsij,rs->ri", tiles, live_mask, precision=lax.Precision.HIGHEST)
    inv_root = 1.0 / jnp.sqrt(degree)
    flat_cols = tile_cols.reshape(slot_total)
    owners = flat_cols // tile_rows
    local_ids = flat_cols % tile_rows
    owner_hot = (owners[:, None] == jnp.arange(devices_all)[None, :]).astype(jnp.int32)
    ranks_seen = jnp.sum(jnp.cumsum(owner_hot, axis=0) * owner_hot, axis=1) - 1
    place = jnp.clip(ranks_seen, 0, REMOTE - 1)
    target = jnp.where(owners == own_index, devices_all, owners)
    wanted = (
        jnp.zeros((devices_all, REMOTE), jnp.int32).at[target, place].set(local_ids, mode="drop")
    )
    asked = lax.all_to_all(wanted, ("row", "grp"), split_axis=0, concat_axis=0, tiled=True)
    tiles_flat = tiles.reshape(slot_total, tile_size, tile_size)
    row_hot = (
        jnp.arange(slot_total)[:, None] // slot_count == jnp.arange(tile_rows)[None, :]
    ).astype(jnp.float32)
    weights_all = row_hot * live_mask.reshape(slot_total)[:, None]
    is_home = owners == own_index
    total_rows = jnp.float32(devices_all * tile_rows * tile_size)
    root_total = jnp.sqrt(total_rows)
    current = block
    factor = None
    for sweep_no in range(ITERS):
        scaled = current.reshape(tile_rows, tile_size, columns) * inv_root[:, :, None]
        replies = scaled[asked]
        received = lax.all_to_all(replies, ("row", "grp"), split_axis=0, concat_axis=0, tiled=True)
        chosen = jnp.where(is_home[:, None, None], scaled[local_ids], received[owners, place])
        summed = weighted_sum(tiles_flat, chosen, weights_all)
        image_tiles = summed * inv_root[:, :, None]
        image = image_tiles.reshape(tile_rows * tile_size, columns)
        partial_gram = jnp.dot(
            image.T, image, precision=lax.Precision.HIGHEST, preferred_element_type=jnp.float32
        )
        gram_sum = lax.psum(partial_gram, ("row", "grp"))
        factor = jnp.linalg.cholesky(gram_sum)
        current = (
            lax.linalg.triangular_solve(
                factor, image, left_side=False, lower=True, transpose_a=True
            )
            * root_total
        )
    return current


def solution(mesh):
    in_specs = (
        P(("row", "grp"), None, None, None),
        P(("row", "grp"), None),
        P(("row", "grp")),
        P(("row", "grp"), None),
    )
    out_specs = P(("row", "grp"), None)
    return jax.shard_map(
        per_device, mesh=mesh, in_specs=in_specs, out_specs=out_specs, check_vma=False
    )
```

profile of v0, /device:TPU:1, one launch (start us, length us, event | category | flops | bytes accessed | tf_op | source)
XLA Modules:
  0.0 798.2 jit_solution(16191401176148462029)
XLA Ops:
  9.0 2.9 scatter_custom_fusion
  12.6 11.5 %all-to-all-start = ((s32[128,1,1]{2,1,0:T(1,128)}), s32[128,1,1]{2,1,0:T(1,128)S(1)}, u32[]{:S(2)}, u32[]{:S(2)}) async-start(s32[128,1,1]{2,1,0:T(1,128)} %copy.60), calls=%async_computation | async-start | bytes 131072 | tf_op jit(solution)/shard_map/all_to_all | solution.py:35
  24.9 10.2 %reduce_sum.18 = f32[16,20,128]{2,1,0:T(8,128)S(1)} reduce(f32[16,20,128,128]{3,2,1,0:T(8,128)} %param.7, f32[]{:T(128)} %constant.94.clone.1), dimensions={3}, to_apply=%region_0.0 | reduce | flops 5201920 | bytes 21135364 | tf_op jit(solution)/shard_map/rsij,rs->ri/reduce_sum | solution.py:23
  36.3 2.4 fusion.42
  38.7 4.4 gather_fusion.1
  43.0 10.2 %all-to-all-start.1 = ((f32[128,1,128,128]{3,2,1,0:T(8,128)}), f32[128,1,128,128]{3,2,1,0:T(8,128)}, u32[]{:S(2)}, u32[]{:S(2)}) async-start(f32[128,1,128,128]{3,2,1,0:T(8,128)} %bitcast.89), calls=%async_computation.1 | async-start | bytes 16777216 | tf_op jit(solution)/shard_map/all_to_all | solution.py:49
  53.6 8.7 %gather_fusion = f32[320,128,128]{2,1,0:T(8,128)} fusion(f32[16,128,128]{2,1,0:T(8,128)S(1)} %copy.57, s32[1024]{0:T(1024)S(1)} %pad_clamp_fusion.1), kind=kCustom, calls=%fused_computation | custom fusion | bytes 41944320 | tf_op jit(solution)/shard_map/gather | solution.py:50
  62.3 94.8 %all-to-all-done.1 = f32[128,1,128,128]{3,2,1,0:T(8,128)} async-done(((f32[128,1,128,128]{3,2,1,0:T(8,128)}), f32[128,1,128,128]{3,2,1,0:T(8,128)}, u32[]{:S(2)}, u32[]{:S(2)}) %all-to-all-start.1) | async-done | bytes 8388640 | tf_op jit(solution)/shard_map/all_to_all | solution.py:49
  157.1 21.6 %gather_fusion.2 = f32[320,128,128]{2,1,0:T(8,128)} fusion(f32[128,1,128,128]{3,2,1,0:T(8,128)} %all-to-all-done.1, s32[320]{0:T(512)S(1)} %get-tuple-element.6), kind=kCustom, calls=%fused_computation.2 | custom fusion | bytes 41945600 | tf_op jit(solution)/shard_map/gather | solution.py:50
  178.7 47.5 %fusion.6 = f32[320,128,128]{2,1,0:T(8,128)} fusion(f32[320,128,128]{2,1,0:T(8,128)} %bitcast.87, f32[320,128,128]{2,1,0:T(8,128)} %gather_fusion, f32[320,128,128]{2,1,0:T(8,128)} %gather_fusion.2, pred[320]{0:T(512)(128)(4,1)S(1)} %get-tuple-element.9), kind=kOutput, calls=%fused_computation.13 | convolution fusion | flops 8058306560 | bytes 83886400 | tf_op jit(solution)/shard_map/sij,sjk,st->tik/dot_general | solution.py:11
  226.2 28.0 %fusion.22 = f32[16,128,128]{1,0,2:T(8,128)S(1)} fusion(f32[320,128,128]{2,1,0:T(8,128)} %fusion.6, f32[16,128]{1,0:T(8,128)S(1)} %sqrt.3, f32[320]{0:T(512)S(1)} %reshape.312, s32[320]{0:T(512)S(1)} %add_select_fusion), kind=kOutput, calls=%fused_computation.25 | convolution fusion | flops 1006905344 | bytes 22030848 | tf_op jit(solution)/shard_map/sij,sjk,st->tik/dot_general | solution.py:11
  256.4 133.9 %all-reduce.4.cloned.1.call-done = f32[128,128]{0,1:T(8,128)} async-done(((f32[128,128]{0,1:T(8,128)}), f32[128,128]{0,1:T(8,128)}) %all-reduce.4.cloned.1.call-update) | async-done | bytes 65552 | tf_op jit(solution)/shard_map/psum | solution.py:57
  392.0 11.7 %cholesky.44 = f32[128,128]{1,0:T(8,128)S(1)} custom-call(f32[128,128]{1,0:T(8,128)S(1)} %fusion.39), custom_call_target="Cholesky" | custom-call | tf_op jit(solution)/shard_map/jit(cholesky)/cholesky | solution.py:58
  405.1 9.8 %custom-call.10 = f32[1,128,128]{1,2,0:T(8,128)S(1)} custom-call(f32[1,128,128]{2,1,0:T(8,128)S(1)} %fusion.34), custom_call_target="InvertDiagBlocksLowerTriangular" | custom-call | tf_op jit(solution)/shard_map/triangular_solve/custom-call.0 | solution.py:60
  416.9 4.4 gather_fusion.4
  421.2 5.6 all-to-all-start.2
  426.9 8.8 %gather_fusion.3 = f32[320,128,128]{2,1,0:T(8,128)} fusion(f32[16,128,128]{2,1,0:T(8,128)S(1)} %copy.69, s32[1024]{0:T(1024)S(1)} %pad_clamp_fusion.1), kind=kCustom, calls=%fused_computation.3 | custom fusion | bytes 41944320 | tf_op jit(solution)/shard_map/gather | solution.py:50
  435.7 95.0 %all-to-all-done.2 = f32[128,1,128,128]{3,2,1,0:T(8,128)} async-done(((f32[128,1,128,128]{3,2,1,0:T(8,128)}), f32[128,1,128,128]{3,2,1,0:T(8,128)}, u32[]{:S(2)}, u32[]{:S(2)}) %all-to-all-start.2) | async-done | bytes 8388640 | tf_op jit(solution)/shard_map/all_to_all | solution.py:49
  530.6 21.6 %gather_fusion.5 = f32[320,128,128]{2,1,0:T(8,128)} fusion(f32[128,1,128,128]{3,2,1,0:T(8,128)} %all-to-all-done.2, s32[320]{0:T(512)S(1)} %get-tuple-element.6), kind=kCustom, calls=%fused_computation.5 | custom fusion | bytes 41945600 | tf_op jit(solution)/shard_map/gather | solution.py:50
  552.3 47.5 %fusion.4 = f32[320,128,128]{2,1,0:T(8,128)} fusion(f32[320,128,128]{2,1,0:T(8,128)} %bitcast.88, f32[320,128,128]{2,1,0:T(8,128)} %gather_fusion.3, f32[320,128,128]{2,1,0:T(8,128)} %gather_fusion.5, pred[320]{0:T(512)(128)(4,1)S(1)} %get-tuple-element.9), kind=kOutput, calls=%fused_computation.11 | convolution fusion | flops 8058306560 | bytes 83886400 | tf_op jit(solution)/shard_map/sij,sjk,st->tik/dot_general | solution.py:11
  599.7 27.8 %fusion.19 = f32[16,128,128]{1,0,2:T(8,128)S(1)} fusion(f32[320,128,128]{2,1,0:T(8,128)} %fusion.4, f32[16,128]{1,0:T(8,128)S(1)} %sqrt.3, f32[320]{0:T(512)S(1)} %reshape.312, s32[320]{0:T(512)S(1)} %add_select_fusion), kind=kOutput, calls=%fused_computation.24 | convolution fusion | flops 1006905344 | bytes 22030848 | tf_op jit(solution)/shard_map/sij,sjk,st->tik/dot_general | solution.py:11
  629.7 133.9 %all-reduce.6.cloned.1.call-done = f32[128,128]{0,1:T(8,128)} async-done(((f32[128,128]{0,1:T(8,128)}), f32[128,128]{0,1:T(8,128)}) %all-reduce.6.cloned.1.call-update) | async-done | bytes 65552 | tf_op jit(solution)/shard_map/psum | solution.py:57
  765.5 11.7 %cholesky.55 = f32[128,128]{1,0:T(8,128)S(1)} custom-call(f32[128,128]{1,0:T(8,128)S(1)} %fusion.37), custom_call_target="Cholesky" | custom-call | tf_op jit(solution)/shard_map/jit(cholesky)/cholesky | solution.py:58
  778.5 9.8 %custom-call.11 = f32[1,128,128]{1,2,0:T(8,128)S(1)} custom-call(f32[1,128,128]{2,1,0:T(8,128)S(1)} %fusion.35), custom_call_target="InvertDiagBlocksLowerTriangular" | custom-call | tf_op jit(solution)/shard_map/triangular_solve/custom-call.0 | solution.py:60
  (52 shorter events, 20.5 us)
Async XLA Ops:
  6.5 28.7 %copy-start = (f32[2048,128]{1,0:T(8,128)S(1)}, f32[2048,128]{1,0:T(8,128)}, u32[]{:S(2)}) copy-start(f32[2048,128]{1,0:T(8,128)} %param.10) | copy-start | bytes 3145732
  12.6 23.7 %all-to-all-start = ((s32[128,1,1]{2,1,0:T(1,128)}), s32[128,1,1]{2,1,0:T(1,128)S(1)}, u32[]{:S(2)}, u32[]{:S(2)}) async-start(s32[128,1,1]{2,1,0:T(1,128)} %copy.60), calls=%async_computation | async-start | bytes 131072 | tf_op jit(solution)/shard_map/all_to_all | solution.py:35
  43.0 114.1 %all-to-all-start.1 = ((f32[128,1,128,128]{3,2,1,0:T(8,128)}), f32[128,1,128,128]{3,2,1,0:T(8,128)}, u32[]{:S(2)}, u32[]{:S(2)}) async-start(f32[128,1,128,128]{3,2,1,0:T(8,128)} %bitcast.89), calls=%async_computation.1 | async-start | bytes 16777216 | tf_op jit(solution)/shard_map/all_to_all | solution.py:49
  53.3 336.9 %all-reduce.4.cloned.1.call-start = ((), (), s32[]{:S(2)}) async-start(), calls=%async_computation.3 | async-start | bytes 131072 | tf_op jit(solution)/shard_map/psum | solution.py:57
  421.2 109.4 %all-to-all-start.2 = ((f32[128,1,128,128]{3,2,1,0:T(8,128)}), f32[128,1,128,128]{3,2,1,0:T(8,128)}, u32[]{:S(2)}, u32[]{:S(2)}) async-start(f32[128,1,128,128]{3,2,1,0:T(8,128)} %bitcast.90), calls=%async_computation.2 | async-start | bytes 16777216 | tf_op jit(solution)/shard_map/all_to_all | solution.py:49
  426.8 336.9 %all-reduce.6.cloned.1.call-start = ((), (), s32[]{:S(2)}) async-start(), calls=%async_computation.4 | async-start | bytes 131072 | tf_op jit(solution)/shard_map/psum | solution.py:57
Sparse Core Ops, SparseCore 0:
  256.5 133.6 all-reduce.3
  629.9 133.7 all-reduce.5
where the time goes:
time: 805 us; the launch traced here: 798 us
  waiting for transfers between devices  458 us (57%)
  matrix products  158 us (20%)
  local copies, waits for them, and re-layouts  79.5 us (10%)
  other arithmetic  61.5 us (8%)
  starting transfers between devices  27.5 us (3%)
  between operations  14.1 us (2%)
    psum x2, waiting for transfers between devices, per_device(): gram_sum = lax.psum(partial_gram, ('row', 'grp'))  268 us
    all_to_all x2, waiting for transfers between devices, per_device(): lax.all_to_all(replies, ('row', 'grp'), split_axis=0, concat_axis=0, tile...  190 us
    dot_general x4, matrix products, weighted_sum(): jnp.einsum('sij,sjk,st->tik', tile_set, vectors, weights, precision=lax.P...  151 us
    gather x2, local copies, waits for them, and re-layouts, per_device(): received[owners, place]  43.2 us
    another operation x6, other arithmetic, per_device(): factor = jnp.linalg.cholesky(gram_sum)  24.8 us
    another operation x4, other arithmetic, per_device(): lax.linalg.triangular_solve(factor, image, left_side=False, lower=True, t...  20.9 us
    gather x2, local copies, waits for them, and re-layouts, per_device(): scaled[local_ids]  17.5 us
  transfers between devices with their start and end apart: 5, of which 4 were waited for; matrix products, arithmetic and copies ran while one was open for 4% of the time, Pallas kernels for 0%

commit v1 on v0

v1 whole, which is shorter than its diff:
```python
import functools

import jax
import jax.numpy as jnp
from jax import lax
from jax.experimental import pallas as pl
from jax.experimental.pallas import tpu as pltpu
from jax.sharding import PartitionSpec as P

MESH = pl.DeviceIdType.MESH
T = 128
ROWS = 16
SLOTS = 20
ITERS = 2
PARTS = (48, 40, 40)
STARTS = (0, 48, 88)
ORDERS = (("z", "x", "y"), ("y", "z", "x"), ("x", "y", "z"))
STEPS = (1, 3, 2)
HIGH = lax.Precision.HIGHEST
F32 = jnp.float32


def split(a):
    hi = a.astype(jnp.bfloat16)
    return hi, (a - hi.astype(F32)).astype(jnp.bfloat16)


def product(a, b):
    ah, al = split(a)
    bh, bl = split(b)
    dot = functools.partial(jnp.dot, preferred_element_type=F32)
    return dot(ah, bh) + (dot(ah, bl) + dot(al, bh))


def inverse_factor(m_ref, v_ref):
    lane = lax.broadcasted_iota(jnp.int32, (8, T), 1)
    sub = lax.broadcasted_iota(jnp.int32, (8, T), 0)
    v_ref[...] = (
        lax.broadcasted_iota(jnp.int32, (T, T), 0) == lax.broadcasted_iota(jnp.int32, (T, T), 1)
    ).astype(F32)

    def block(b, carry):
        base = pl.multiple_of(b * 8, 8)
        p = m_ref[pl.ds(base, 8), :]
        q = v_ref[pl.ds(base, 8), :]
        for j in range(8):
            col = jnp.sum(jnp.where(lane == base + j, p, 0.0), axis=1, keepdims=True)
            scale = 1.0 / jnp.sqrt(col[j : j + 1, :])
            prow = p[j : j + 1, :] * scale
            qrow = q[j : j + 1, :] * scale
            coef = jnp.where(sub > j, col * scale, 0.0)
            p = jnp.where(sub == j, prow, p - coef * prow)
            q = jnp.where(sub == j, qrow, q - coef * qrow)
        v_ref[pl.ds(base, 8), :] = q
        below = jnp.where(lane >= base + 8, p, 0.0)
        both = jnp.concatenate([p, q], axis=1)
        update = lax.dot_general(
            below, both, (((0,), (0,)), ((), ())), precision=HIGH, preferred_element_type=F32
        )
        m_ref[...] -= update[:, :T]
        v_ref[...] -= update[:, T:]
        return carry

    lax.fori_loop(0, T // 8, block, 0)


def kernel(
    tiles_hbm, block_ref, want_ref, slot_ref, own_ref, far_ref, live_ref, out_ref,
    tiles, ag0, ag1, ag2, ag3, ag4, ag5, ag6, ag7, ag8, ag9, ag10, ag11, st0, st1, st2, xr0, xr1, xr2, fn0, fn1, fn2,
    scaled, acc, inv, sums, gram, factor, wtab, stab,
    load_sem, s1s, s1r, s2s, s2r, s3s, s3r, loc_sem, ws, wr, tab_sem, gs, gr, free_in, free_out,
):
    ag = ((ag0, ag1, ag2, ag3), (ag4, ag5, ag6, ag7), (ag8, ag9, ag10, ag11))
    st, xr, fn = (st0, st1, st2), (xr0, xr1, xr2), (fn0, fn1, fn2)
    row, grp = lax.axis_index("row"), lax.axis_index("grp")
    at = {"z": row // 8, "y": (row // 2) % 4, "x": grp, "c": row % 2}

    def device(**by):
        v = {k: lax.rem(at[k] + by[k], 2 if k == "c" else 4) if k in by else at[k] for k in at}
        return (v["z"] * 8 + v["y"] * 2 + v["c"], v["x"])

    for r in range(ROWS):
        pltpu.make_async_copy(tiles_hbm.at[r], tiles.at[r], load_sem.at[r]).start()

    barrier = pltpu.get_barrier_semaphore()
    same_core = [{a: d} for a in "xyz" for d in STEPS]
    all_peers = same_core + [{a: d, "c": 1} for a in "xyz" for d in STEPS] + [{"c": 1}]
    for by in all_peers:
        pl.semaphore_signal(barrier, inc=1, device_id=device(**by), device_id_type=MESH)
    pl.semaphore_wait(barrier, len(all_peers))

    wtab[0, 0, 0, 0] = want_ref[...]

    def table_copies(stage):
        axis = "zyxc"[stage]
        copies = []
        for d in (1,) if axis == "c" else STEPS:
            src, dst = {
                "z": (wtab.at[0, 0, 0, 0], wtab.at[0, 0, 0, d]),
                "y": (wtab.at[0, 0, 0], wtab.at[0, 0, d]),
                "x": (wtab.at[0, 0], wtab.at[0, d]),
                "c": (wtab.at[0], wtab.at[d]),
            }[axis]
            copies.append(
                pltpu.make_async_remote_copy(
                    src, dst, ws.at[stage, d], wr.at[stage, d], device_id=device(**{axis: d}), device_id_type=MESH
                )
            )
        return copies

    def degree_row(r):
        pltpu.make_async_copy(tiles_hbm.at[r], tiles.at[r], load_sem.at[r]).wait()

        def add(s, total):
            return total + tiles[r, s] * live_ref[r * SLOTS + s]

        total = lax.fori_loop(0, SLOTS, add, jnp.zeros((T, T), F32), unroll=4)
        root = 1.0 / jnp.sqrt(jnp.sum(total, axis=1, keepdims=True))
        inv[r] = jnp.broadcast_to(root, (T, T))

    for stage in range(4):
        copies = table_copies(stage)
        for copy in copies:
            copy.start()

        def some(r, carry):
            degree_row(r)
            return carry

        lax.fori_loop(stage * 4, stage * 4 + 4, some, 0)
        for copy in copies:
            copy.wait()
    table = pltpu.make_async_copy(wtab, stab, tab_sem)
    table.start()

    scaled[ROWS] = jnp.zeros((T, T), F32)
    for i in range(3):
        fn[i][0, 0] = jnp.zeros((PARTS[i], T), F32)

    def put(r, value):
        scaled[r] = value
        for i in range(3):
            ag[i][0][r] = value[STARTS[i] : STARTS[i] + PARTS[i], :]

    def begin(r, carry):
        put(r, block_ref[r] * inv[r])
        return carry

    lax.fori_loop(0, ROWS, begin, 0)
    table.wait()

    def gather_copy(i, d):
        return pltpu.make_async_remote_copy(
            ag[i][0], ag[i][d], s1s.at[i, d], s1r.at[i, d],
            device_id=device(**{ORDERS[i][0]: d}), device_id_type=MESH,
        )

    def second_copy(i, d2, d1):
        return pltpu.make_async_remote_copy(
            st[i].at[d2 - 1, d1], xr[i].at[d2, d1], s2s.at[i, d2, d1], s2r.at[i, d2, d1],
            device_id=device(**{ORDERS[i][1]: d2}), device_id_type=MESH,
        )

    def select(i, d1):
        a1, a2, a3 = ORDERS[i]
        for d2 in range(4):

            def pick(e, carry):
                d3, dc = e // 2, e % 2
                off = {a1: d1, a2: d2, a3: d3}
                back = {a1: 0, a2: (4 - d2) % 4, a3: lax.rem(4 - d3, 4)}
                place = ((off["x"] * 4 + off["y"]) * 4 + off["z"]) * 2 + dc
                which = stab[dc, back["x"], back["y"], back["z"], 0, place]
                value = ag[i][d1][which]
                if d2 == 0:
                    xr[i][0, d1, e] = value
                else:
                    st[i][d2 - 1, d1, e] = value
                return carry

            lax.fori_loop(0, 8, pick, 0, unroll=4)

    def third_start(i, d2):
        a3 = ORDERS[i][2]
        for e in (2, 6, 3, 7, 4, 5, 1):
            by = {a3: e // 2} if e >= 2 else {}
            if e % 2:
                by["c"] = 1
            pltpu.make_async_remote_copy(
                xr[i].at[d2, :, e], fn[i].at[e, pl.ds(d2 * 4, 4)], s3s.at[i], s3r.at[i],
                device_id=device(**by), device_id_type=MESH,
            ).start()

    def third_all(i):
        return pltpu.make_async_remote_copy(
            fn[i].at[pl.ds(1, 7)], fn[i].at[pl.ds(1, 7)], s3s.at[i], s3r.at[i],
            device_id=device(c=1), device_id_type=MESH,
        )

    def own_copy(i, d2):
        first = 1 if d2 == 0 else 0
        return pltpu.make_async_copy(
            xr[i].at[d2, pl.ds(first, 4 - first), 0],
            fn[i].at[0, pl.ds(d2 * 4 + first, 4 - first)],
            loc_sem.at[i, d2],
        )

    def home(r, carry):
        total = jnp.zeros((T, T), F32)
        for s in range(0, SLOTS, 2):
            a = jnp.concatenate([tiles[r, s], tiles[r, s + 1]], axis=1)
            b = jnp.concatenate([scaled[own_ref[r * SLOTS + s]], scaled[own_ref[r * SLOTS + s + 1]]], axis=0)
            total = total + product(a, b)
        acc[r] = total
        return carry

    def far_places(dx, dy, dz, dc):
        off = {"x": dx, "y": dy, "z": dz}
        return [(off[a3] * 2 + dc, off[a2] * 4 + off[a1]) for a1, a2, a3 in ORDERS]

    def far_products(first, group, carry):
        for lower in range(first, 8):
            places = far_places(group // 4, group % 4, lower // 2, lower % 2)
            slot = slot_ref[group * 8 + lower]
            x = jnp.concatenate([fn[i][places[i]] for i in range(3)], axis=0)
            value = product(tiles[slot // SLOTS, lax.rem(slot, SLOTS)], x)
            for i in range(3):
                fn[i][places[i]] = value[STARTS[i] : STARTS[i] + PARTS[i], :]
        return carry

    def add_far(r):
        total = acc[r]
        pieces = [total[STARTS[i] : STARTS[i] + PARTS[i], :] for i in range(3)]
        for s in range(SLOTS):
            for i in range(3):
                where = far_ref[i, r * SLOTS + s]
                pieces[i] = pieces[i] + fn[i][where // 16, lax.rem(where, 16)]
        return jnp.concatenate(pieces, axis=0) * inv[r]

    def gram_copies(it, stage):
        axis = "cxyz"[stage]
        return [
            pltpu.make_async_remote_copy(
                sums.at[it, stage, 0], sums.at[it, stage, d], gs.at[it, stage, d], gr.at[it, stage, d],
                device_id=device(**{axis: d}), device_id_type=MESH,
            )
            for d in ((1,) if axis == "c" else STEPS)
        ]

    def gram_start(it, stage):
        sums[it, stage, 0] = gram[...]
        for copy in gram_copies(it, stage):
            copy.start()

    def gram_finish(it, stage):
        copies = gram_copies(it, stage)
        for copy in copies:
            copy.wait()
        for d in range(1, len(copies) + 1):
            gram[...] += sums[it, stage, d]

    def local_gram():
        def add(r, total):
            a = acc[r]
            return total + lax.dot_general(
                a, a, (((0,), (0,)), ((), ())), precision=HIGH, preferred_element_type=F32
            )

        gram[...] = lax.fori_loop(0, ROWS, add, jnp.zeros((T, T), F32))

    root_total = jnp.sqrt(F32(ROWS * T * 128))

    def normalised(value):
        return root_total * lax.dot_general(
            value, factor[...], (((1,), (1,)), ((), ())), precision=HIGH, preferred_element_type=F32
        )

    for it in range(ITERS):
        if it:
            pl.semaphore_wait(free_in, len(same_core))
        for d in STEPS:
            for i in range(3):
                gather_copy(i, d).start()
        if it:
            local_gram()
            gram_start(0, 0)
        for d1 in (0, *STEPS):
            for i in range(3):
                if d1:
                    gather_copy(i, d1).wait_recv()
                select(i, d1)
                for d2 in STEPS:
                    second_copy(i, d2, d1).start()
            if it:
                stage = (0, *STEPS).index(d1)
                gram_finish(0, stage)
                if stage < 3:
                    gram_start(0, stage + 1)
        if it:
            pl.semaphore_wait(free_out, len(all_peers))
        for i in range(3):
            third_start(i, 0)
            own_copy(i, 0).start()
        lax.fori_loop(0, ROWS, home, 0)
        if it:
            inverse_factor(gram, factor)
        for d2 in STEPS:
            for i in range(3):
                for d1 in range(4):
                    second_copy(i, d2, d1).wait_recv()
                third_start(i, d2)
                own_copy(i, d2).start()
        for i in range(3):
            for d in STEPS:
                gather_copy(i, d).wait_send()
                for d1 in range(4):
                    second_copy(i, d, d1).wait_send()
            third_all(i).wait_send()
            for d2 in range(4):
                own_copy(i, d2).wait()
        if it == 0:
            for by in same_core:
                pl.semaphore_signal(free_in, inc=1, device_id=device(**by), device_id_type=MESH)
        for i in range(3):
            third_all(i).wait_recv()
        far_products(1, 0, 0)
        lax.fori_loop(1, 16, functools.partial(far_products, 0), 0)

        if it == 0:

            def close(r, carry):
                image = add_far(r)
                acc[r] = image
                put(r, image * inv[r])
                return carry

            lax.fori_loop(0, ROWS, close, 0)
            for by in all_peers:
                pl.semaphore_signal(free_out, inc=1, device_id=device(**by), device_id_type=MESH)
        else:

            def close_last(r, carry):
                acc[r] = normalised(add_far(r))
                return carry

            lax.fori_loop(0, ROWS, close_last, 0)
    local_gram()
    for stage in range(4):
        gram_start(1, stage)
        gram_finish(1, stage)
    inverse_factor(gram, factor)

    def finish(r, carry):
        out_ref[r] = normalised(acc[r])
        return carry

    lax.fori_loop(0, ROWS, finish, 0)


def per_device(tiles, tile_cols, tile_counts, block):
    row, grp = lax.axis_index("row"), lax.axis_index("grp")
    me = {"z": row // 8, "y": (row // 2) % 4, "c": row % 2, "x": grp}
    slot = jnp.arange(ROWS * SLOTS, dtype=jnp.int32)
    cols = tile_cols.reshape(ROWS * SLOTS)
    owner, local = cols // ROWS, cols % ROWS
    live = (jnp.arange(SLOTS)[None, :] < tile_counts[:, None]).reshape(ROWS * SLOTS)
    away = {
        "x": (me["x"] - owner) % 4,
        "c": (me["c"] - owner // 4) % 2,
        "y": (me["y"] - owner // 8) % 4,
        "z": (me["z"] - owner // 32) % 4,
    }
    place = ((away["x"] * 4 + away["y"]) * 4 + away["z"]) * 2 + away["c"]
    far = place > 0
    hot = (place[:, None] == jnp.arange(128)[None, :]) & far[:, None]
    want = jnp.sum(jnp.where(hot, local[:, None], 0), axis=0).reshape(1, 128)
    far_slot = jnp.sum(jnp.where(hot, slot[:, None], 0), axis=0)
    own = jnp.where(live & ~far, local, ROWS)
    far_place = jnp.stack(
        [
            jnp.where(far, ((away[a3] * 2 + away["c"]) * 4 + away[a2]) * 4 + away[a1], 0)
            for a1, a2, a3 in ORDERS
        ]
    )
    smem, vmem = pl.BlockSpec(memory_space=pltpu.SMEM), pl.BlockSpec(memory_space=pltpu.VMEM)
    dma = pltpu.SemaphoreType.DMA
    out = pl.pallas_call(
        kernel,
        out_shape=jax.ShapeDtypeStruct((ROWS, T, T), F32),
        in_specs=[pl.BlockSpec(memory_space=pl.ANY), vmem, vmem, smem, smem, smem, smem],
        out_specs=vmem,
        scratch_shapes=[
            pltpu.VMEM((ROWS, SLOTS, T, T), F32),
            *[pltpu.VMEM((ROWS, n, T), F32) for n in PARTS for _ in range(4)],
            *[pltpu.VMEM((3, 4, 8, n, T), F32) for n in PARTS],
            *[pltpu.VMEM((4, 4, 8, n, T), F32) for n in PARTS],
            *[pltpu.VMEM((8, 16, n, T), F32) for n in PARTS],
            pltpu.VMEM((ROWS + 1, T, T), F32),
            pltpu.VMEM((ROWS, T, T), F32),
            pltpu.VMEM((ROWS, T, T), F32),
            pltpu.VMEM((2, 4, 4, T, T), F32),
            pltpu.VMEM((T, T), F32),
            pltpu.VMEM((T, T), F32),
            pltpu.VMEM((2, 4, 4, 4, 1, T), jnp.int32),
            pltpu.SMEM((2, 4, 4, 4, 1, T), jnp.int32),
            dma((ROWS,)),
            dma((3, 4)),
            dma((3, 4)),
            dma((3, 4, 4)),
            dma((3, 4, 4)),
            dma((3,)),
            dma((3,)),
            dma((3, 4)),
            dma((4, 4)),
            dma((4, 4)),
            dma,
            dma((2, 4, 4)),
            dma((2, 4, 4)),
            pltpu.SemaphoreType.REGULAR,
            pltpu.SemaphoreType.REGULAR,
        ],
        compiler_params=pltpu.CompilerParams(
            collective_id=0, has_side_effects=True, vmem_limit_bytes=60 * 2**20
        ),
    )(
        tiles, block.reshape(ROWS, T, T), want.astype(jnp.int32), far_slot.astype(jnp.int32),
        own.astype(jnp.int32), far_place.astype(jnp.int32), live.astype(F32),
    )
    return out.reshape(ROWS * T, T)


def solution(mesh):
    shard = ("row", "grp")
    return jax.shard_map(
        per_device,
        mesh=mesh,
        in_specs=(P(shard, None, None, None), P(shard, None), P(shard), P(shard, None)),
        out_specs=P(shard, None),
        check_vma=False,
    )
```

time: 805 us -> 280 us (0.35)
  waiting for transfers between devices: 458 us -> 0 us
  Pallas kernels: 0 us -> 271 us
  matrix products: 158 us -> 0 us
  local copies, waits for them, and re-layouts: 79.5 us -> 3.92 us
  other arithmetic: 61.5 us -> 3.42 us
  starting transfers between devices: 27.5 us -> 0 us
  between operations: 14.1 us -> 0.03 us
    pallas_call x0 -> x1, Pallas kernels: none -> 271 us  [per_device(): pl.pallas_call(kernel, out_shape=jax.ShapeDtypeStruct((ROWS, T, T), F32),...]
    psum x2 -> x0, waiting for transfers between devices: 268 us -> none  [per_device(): gram_sum = lax.psum(partial_gram, ('row', 'grp'))]
    all_to_all x3 -> x0, waiting for transfers between devices: 190 us -> none  [the longest x2 190 us: per_device(): lax.all_to_all(replies, ('row', 'grp'), split_axis=0, concat_axis=0, tile...]
    dot_general x7 -> x0, matrix products: 155 us -> none  [the longest x4 151 us: weighted_sum(): jnp.einsum('sij,sjk,st->tik', tile_set, vectors, weights, precision=lax.P...]
    gather x6 -> x0, local copies, waits for them, and re-layouts: 69.4 us -> none  [the longest x2 43.2 us: per_device(): received[owners, place]]
    another operation x14 -> x1, other arithmetic: 45.9 us -> 0.6 us  [per_device(): jnp.stack([jnp.where(far, ((away[a3] * 2 + away['c']) * 4 + away[a2]) * 4...]
    all_to_all x3 -> x0, starting transfers between devices: 27.3 us -> none  [the longest x2 15.8 us: per_device(): lax.all_to_all(replies, ('row', 'grp'), split_axis=0, concat_axis=0, tile...]
    reduce_sum x2 -> x1, other arithmetic: 10.4 us -> 0.78 us  [per_device(): far_slot = jnp.sum(jnp.where(hot, slot[:, None], 0), axis=0)]
  transfers between devices with their start and end apart: 5 -> 0, of which waited for: 4 -> 0; matrix products, arithmetic and copies ran while one was open for 4% -> 0% of each run, Pallas kernels for 0% -> 0%
where the time goes in v1:
time: 280 us; the launch traced here: 278 us
  Pallas kernels  271 us (97%)
  local copies, waits for them, and re-layouts  3.92 us (1%)
  other arithmetic  3.42 us (1%)
    pallas_call x1, Pallas kernels, per_device(): pl.pallas_call(kernel, out_shape=jax.ShapeDtypeStruct((ROWS, T, T), F32),...  271 us

profile of v1, /device:TPU:1, one launch (start us, length us, event | category | flops | bytes accessed | tf_op | source)
XLA Modules:
  0.0 278.5 jit_solution(16209261469241440418)
XLA Ops:
  0.0 0.8 reshape.599
  0.8 0.7 iota_compare_fusion.1
  1.5 0.1 lt.67
  1.6 0.6 convert_element_type.3.live_ref
  2.2 0.8 reshape.597
  3.0 0.6 and_select_fusion.8
  3.6 0.8 select_reduce_fusion
  4.4 0.1 add_select_fusion.11
  4.5 0.6 pad_add_fusion.far_ref
  5.1 271.1 %shard_map.46 = f32[16,128,128]{2,1,0:T(8,128)} custom-call(f32[16,20,128,128]{3,2,1,0:T(8,128)} %tiles_hbm.1, f32[16,128,128]{2,1,0:T(8,128)} %bitcast.4, s32[1,128]{1,0:T(1,128)} %bitcast.5, s32[128]{0:T(128)} %get-tuple-element.5.slot_ref, s32[320]{0:T(512)} %get-tuple-element.12.own_ref, s32[3,320]{1,0:T(4,128)} %pad_add_fusion.far_ref, ...), custom_call_target="tpu_custom_call" | custom-call | tf_op jit(solution)/shard_map/pallas_call | solution.py:387
  276.2 2.3 copy.6
  (1 shorter events, 0.0 us)

commit v2 on v1

v2 whole, which is shorter than its diff:
```python
import functools

import jax
import jax.numpy as jnp
from jax import lax
from jax.experimental import pallas as pl
from jax.experimental.pallas import tpu as pltpu
from jax.sharding import PartitionSpec as P

MESH = pl.DeviceIdType.MESH
T = 128
ROWS = 16
SLOTS = 20
ITERS = 2
PARTS = (48, 40, 40)
STARTS = (0, 48, 88)
ORDERS = (("z", "x", "y"), ("y", "z", "x"), ("x", "y", "z"))
STEPS = (1, 3, 2)
FAR_STEP = 8
STAGED = 6
HIGH = lax.Precision.HIGHEST
F32 = jnp.float32


def split(a):
    hi = a.astype(jnp.bfloat16)
    return hi, (a - hi.astype(F32)).astype(jnp.bfloat16)


def inverse_factor(m_ref, v_ref):
    lane = lax.broadcasted_iota(jnp.int32, (8, T), 1)
    sub = lax.broadcasted_iota(jnp.int32, (8, T), 0)
    v_ref[...] = (
        lax.broadcasted_iota(jnp.int32, (T, T), 0) == lax.broadcasted_iota(jnp.int32, (T, T), 1)
    ).astype(F32)

    def block(b, carry):
        base = pl.multiple_of(b * 8, 8)
        p = m_ref[pl.ds(base, 8), :]
        q = v_ref[pl.ds(base, 8), :]
        cols = [
            jnp.broadcast_to(jnp.sum(jnp.where(lane == base + j, p, 0.0), axis=1, keepdims=True), (8, T))
            for j in range(8)
        ]
        for j in range(8):
            pivot = jnp.broadcast_to(cols[j][j : j + 1, :], (8, T))
            scale = lax.rsqrt(pivot)
            scale = scale * (1.5 - 0.5 * pivot * scale * scale)
            coef = jnp.where(sub > j, cols[j] * scale, 0.0)
            for m in range(j + 1, 8):
                cols[m] = cols[m] - coef * (jnp.broadcast_to(cols[m][j : j + 1, :], (8, T)) * scale)
            prow = jnp.broadcast_to(p[j : j + 1, :], (8, T)) * scale
            qrow = jnp.broadcast_to(q[j : j + 1, :], (8, T)) * scale
            p = jnp.where(sub == j, prow, p - coef * prow)
            q = jnp.where(sub == j, qrow, q - coef * qrow)
        v_ref[pl.ds(base, 8), :] = q
        below = jnp.where(lane >= base + 8, p, 0.0)
        both = jnp.concatenate([p, q], axis=1)
        update = lax.dot_general(
            below, both, (((0,), (0,)), ((), ())), precision=HIGH, preferred_element_type=F32
        )
        m_ref[...] -= update[:, :T]
        v_ref[...] -= update[:, T:]
        return carry

    lax.fori_loop(0, T // 8, block, 0)


def index_kernel(cols_ref, counts_ref, want_ref, own_ref, slot_ref, place_ref, keep_ref, last_ref):
    row, x = lax.axis_index("row"), lax.axis_index("grp")
    z, y, c = row // 8, (row // 2) % 4, row % 2
    want_ref[0, 0] = 0
    slot_ref[127] = 0
    keep_ref[127] = 0
    for i in range(3):
        place_ref[i, 127] = 0

    def one_row(r, first):
        last_ref[r] = 127
        count = counts_ref[r]

        def one_slot(s, n):
            col = cols_ref[r, s]
            owner, local = col >> 4, col & 15
            away = {"x": (x - owner) & 3, "y": (y - (owner >> 3)) & 3, "z": (z - (owner >> 5)) & 3}
            dc = (c - (owner >> 2)) & 1
            place = away["x"] * 32 + away["y"] * 8 + away["z"] * 2 + dc
            far = place != 0
            k = r * SLOTS + s
            own_ref[k] = jnp.where(far | (s >= count), ROWS, local)

            @pl.when(far)
            def _():
                want_ref[0, place] = local
                slot_ref[n] = k
                for i, (a1, a2, a3) in enumerate(ORDERS):
                    place_ref[i, n] = (away[a3] * 2 + dc) * 16 + away[a2] * 4 + away[a1]
                keep_ref[n] = jnp.where(n == first, 0, 1)
                last_ref[r] = n

            return n + far.astype(jnp.int32)

        return lax.fori_loop(0, SLOTS, one_slot, first)

    lax.fori_loop(0, ROWS, one_row, jnp.int32(0))


def kernel(
    tiles_hbm, block_ref, want_ref, own_ref, slot_ref, place_ref, keep_ref, last_ref, counts_ref, out_ref,
    whi, wlo, work, ag1, ag2, ag3, ag4, ag5, ag6, ag7, ag8, ag9,
    st0, st1, st2, xr0, xr1, xr2, fn0, fn1, fn2, xs, xcat, inv, icol, ic0, ic1, ic2,
    gsrc, gpart, gline, gout, factor, wtab, stab,
    load_sem, s1s, s1r, fs, fr, is_, ir, s2s, s2r, s3s, s3r, loc_sem, ws, wr, tab_sem, gs, gr, free_in, free_out,
):
    ag = ((None, ag1, ag2, ag3), (None, ag4, ag5, ag6), (None, ag7, ag8, ag9))
    st, xr, fn, ic = (st0, st1, st2), (xr0, xr1, xr2), (fn0, fn1, fn2), (ic0, ic1, ic2)
    acc = out_ref
    row, grp = lax.axis_index("row"), lax.axis_index("grp")
    at = {"z": row // 8, "y": (row // 2) % 4, "x": grp, "c": row % 2}

    def device(**by):
        v = {k: lax.rem(at[k] + by[k], 2 if k == "c" else 4) if k in by else at[k] for k in at}
        return (v["z"] * 8 + v["y"] * 2 + v["c"], v["x"])

    def load_copy(r):
        place = pl.multiple_of(lax.rem(r, STAGED) * SLOTS, SLOTS)
        return pltpu.make_async_copy(tiles_hbm.at[r], work.at[pl.ds(place, SLOTS)], load_sem.at[r])

    for r in range(STAGED):
        load_copy(r).start()

    barrier = pltpu.get_barrier_semaphore()
    same_core = [{a: d} for a in "xyz" for d in STEPS]
    all_peers = same_core + [{a: d, "c": 1} for a in "xyz" for d in STEPS] + [{"c": 1}]
    for by in all_peers:
        pl.semaphore_signal(barrier, inc=1, device_id=device(**by), device_id_type=MESH)
    pl.semaphore_wait(barrier, len(all_peers))

    def gather_copy(i, d, it):
        source = xs if it else block_ref
        return pltpu.make_async_remote_copy(
            source.at[:, pl.ds(STARTS[i], PARTS[i])], ag[i][d], s1s.at[i, d], s1r.at[i, d],
            device_id=device(**{ORDERS[i][0]: d}), device_id_type=MESH,
        )

    half = ROWS // 2

    def forward_copy(i, d):
        part = pl.ds(0 if d == 1 else half, half)
        return pltpu.make_async_remote_copy(
            ag[i][d].at[part], ag[i][2].at[part], fs.at[i, d], fr.at[i, d],
            device_id=device(**{ORDERS[i][0]: d}), device_id_type=MESH,
        )

    def root_copy(i, d):
        return pltpu.make_async_remote_copy(
            icol.at[pl.ds(STARTS[i], PARTS[i])], ic[i].at[d], is_.at[i, d], ir.at[i, d],
            device_id=device(**{ORDERS[i][0]: d}), device_id_type=MESH,
        )

    wtab[0, 0, 0, 0] = want_ref[...]

    def table_copies(stage):
        axis = "zyxc"[stage]
        copies = []
        for d in (1,) if axis == "c" else STEPS:
            src, dst = {
                "z": (wtab.at[0, 0, 0, 0], wtab.at[0, 0, 0, d]),
                "y": (wtab.at[0, 0, 0], wtab.at[0, 0, d]),
                "x": (wtab.at[0, 0], wtab.at[0, d]),
                "c": (wtab.at[0], wtab.at[d]),
            }[axis]
            copies.append(
                pltpu.make_async_remote_copy(
                    src, dst, ws.at[stage, d], wr.at[stage, d], device_id=device(**{axis: d}), device_id_type=MESH
                )
            )
        return copies

    lane = lax.broadcasted_iota(jnp.int32, (T, T), 1)

    def take_row(r, columns):
        load_copy(r).wait()
        place = lax.rem(r, STAGED) * SLOTS
        count = counts_ref[r]

        def add(s, total):
            tile = work[place + s]
            hi, lo = split(tile)
            whi[r, s] = hi
            wlo[r, s] = lo
            return total + tile * jnp.where(s < count, 1.0, 0.0)

        total = lax.fori_loop(0, SLOTS, add, jnp.zeros((T, T), F32), unroll=4)
        root = 1.0 / jnp.sqrt(jnp.sum(total, axis=1, keepdims=True))
        inv[r] = jnp.broadcast_to(root, (T, T))
        return jnp.where(lane == r, root, columns)

    def take_and_load(r, columns):
        columns = take_row(r, columns)
        load_copy(r + STAGED).start()
        return columns

    columns = jnp.zeros((T, T), F32)
    for stage in range(4):
        copies = table_copies(stage)
        for copy in copies:
            copy.start()
        if stage == 0:
            for d in (1, 3):
                for i in range(3):
                    gather_copy(i, d, 0).start()
        low, high = stage * 4, stage * 4 + 4
        middle = min(max(ROWS - STAGED, low), high)
        columns = lax.fori_loop(low, middle, take_and_load, columns)
        columns = lax.fori_loop(middle, high, take_row, columns)
        for copy in copies:
            copy.wait()
    icol[...] = columns
    for d in STEPS:
        for i in range(3):
            root_copy(i, d).start()
    table = pltpu.make_async_copy(wtab, stab, tab_sem)
    table.start()

    xcat[ROWS] = jnp.zeros((T, 2 * T), jnp.bfloat16)
    for i in range(3):
        fn[i][0, 0] = jnp.zeros((PARTS[i], T), F32)

    def put(r, value):
        xs[r] = value
        xcat[r] = jnp.concatenate(split(value), axis=1)

    def begin(r, carry):
        put(r, block_ref[r] * inv[r])
        return carry

    lax.fori_loop(0, ROWS, begin, 0)
    table.wait()

    def second_copy(i, d2, d1):
        return pltpu.make_async_remote_copy(
            st[i].at[d2 - 1, d1], xr[i].at[d2, d1], s2s.at[i, d2, d1], s2r.at[i, d2, d1],
            device_id=device(**{ORDERS[i][1]: d2}), device_id_type=MESH,
        )

    def select(i, d1, it):
        a1, a2, a3 = ORDERS[i]
        for d2 in range(4):

            def pick(e, carry):
                d3, dc = e // 2, e % 2
                off = {a1: d1, a2: d2, a3: d3}
                back = {a1: 0, a2: (4 - d2) % 4, a3: lax.rem(4 - d3, 4)}
                place = ((off["x"] * 4 + off["y"]) * 4 + off["z"]) * 2 + dc
                which = stab[dc, back["x"], back["y"], back["z"], 0, place]
                if d1 == 0:
                    value = xs[which, STARTS[i] : STARTS[i] + PARTS[i]]
                else:
                    value = ag[i][d1][which]
                if d1 and it == 0:
                    roots = jnp.where(lane[: PARTS[i]] == which, ic[i][d1], 0.0)
                    value = value * jnp.sum(roots, axis=1, keepdims=True)
                if d2 == 0:
                    xr[i][0, d1, e] = value
                else:
                    st[i][d2 - 1, d1, e] = value
                return carry

            lax.fori_loop(0, 8, pick, 0, unroll=4)

    def third_start(i, d2):
        a3 = ORDERS[i][2]
        for e in (2, 6, 3, 7, 4, 5, 1):
            by = {a3: e // 2} if e >= 2 else {}
            if e % 2:
                by["c"] = 1
            pltpu.make_async_remote_copy(
                xr[i].at[d2, :, e], fn[i].at[e, pl.ds(d2 * 4, 4)], s3s.at[i], s3r.at[i],
                device_id=device(**by), device_id_type=MESH,
            ).start()

    def third_all(i):
        return pltpu.make_async_remote_copy(
            fn[i].at[pl.ds(1, 7)], fn[i].at[pl.ds(1, 7)], s3s.at[i], s3r.at[i],
            device_id=device(c=1), device_id_type=MESH,
        )

    def own_copy(i, d2):
        first = 1 if d2 == 0 else 0
        return pltpu.make_async_copy(
            xr[i].at[d2, pl.ds(first, 4 - first), 0],
            fn[i].at[0, pl.ds(d2 * 4 + first, 4 - first)],
            loc_sem.at[i, d2],
        )

    dot = functools.partial(jnp.dot, preferred_element_type=F32)

    def home(r, carry):
        total = jnp.zeros((T, 2 * T), F32)
        small = jnp.zeros((T, T), F32)
        for s in range(0, SLOTS, 2):
            b = jnp.concatenate([xcat[own_ref[r * SLOTS + s]], xcat[own_ref[r * SLOTS + s + 1]]], axis=0)
            total = total + dot(jnp.concatenate([whi[r, s], whi[r, s + 1]], axis=1), b)
            small = small + dot(jnp.concatenate([wlo[r, s], wlo[r, s + 1]], axis=1), b[:, :T])
        acc[r] = total[:, :T] + (total[:, T:] + small)
        return carry

    def far_products(group, running):
        values = []
        for k in range(FAR_STEP):
            k = group * FAR_STEP + k
            slot = slot_ref[k]
            pieces = []
            for i in range(3):
                where = place_ref[i, k]
                pieces.append(fn[i][where // 16, lax.rem(where, 16)])
            hi, lo = split(jnp.concatenate(pieces, axis=0))
            r, s = slot // SLOTS, lax.rem(slot, SLOTS)
            wide = dot(whi[r, s], jnp.concatenate([hi, lo], axis=1))
            values.append(wide[:, :T] + (wide[:, T:] + dot(wlo[r, s], hi)))
        for k in range(FAR_STEP):
            running = jnp.where(keep_ref[group * FAR_STEP + k] > 0, running, 0.0) + values[k]
            work[group * FAR_STEP + k] = running
        return running

    def add_far(r):
        return (acc[r] + work[last_ref[r]]) * inv[r]

    group = [(dx, dc) for dx in range(4) for dc in range(2) if dx or dc]
    mine = pl.multiple_of((at["x"] * 2 + at["c"]) * 16, 16)

    def gram_copies(it, stage):
        copies = []
        if stage in (1, 2):
            axis = "yz"[stage - 1]
            for d in STEPS:
                copies.append(
                    pltpu.make_async_remote_copy(
                        gline.at[it, stage - 1, 0], gline.at[it, stage - 1, d],
                        gs.at[it, stage, d], gr.at[it, stage, d],
                        device_id=device(**{axis: d}), device_id_type=MESH,
                    )
                )
            return copies
        for dx, dc in group:
            by = {k: v for k, v in (("x", dx), ("c", dc)) if v}
            e = dx * 2 + dc
            if stage == 0:
                theirs = lax.rem(at["x"] + dx, 4) * 2 + lax.rem(at["c"] + dc, 2)
                src, dst = gsrc.at[it, pl.ds(pl.multiple_of(theirs * 16, 16), 16)], gpart.at[it, e]
            else:
                src = dst = gout.at[it, pl.ds(mine, 16)]
            copies.append(
                pltpu.make_async_remote_copy(
                    src, dst, gs.at[it, stage, e], gr.at[it, stage, e], device_id=device(**by), device_id_type=MESH
                )
            )
        return copies

    def gram_start(it, stage):
        for copy in gram_copies(it, stage):
            copy.start()

    def gram_finish(it, stage):
        for copy in gram_copies(it, stage):
            copy.wait()
        if stage == 0:
            total = gsrc[it, pl.ds(mine, 16)]
            for dx, dc in group:
                total = total + gpart[it, dx * 2 + dc]
        elif stage < 3:
            total = (gline[it, stage - 1, 0] + gline[it, stage - 1, 1]) + (gline[it, stage - 1, 2] + gline[it, stage - 1, 3])
        if stage < 2:
            gline[it, stage, 0] = total
        elif stage == 2:
            gout[it, pl.ds(mine, 16)] = total

    def local_gram(it):
        def add(r, total):
            a = acc[r]
            return total + lax.dot_general(
                a, a, (((0,), (0,)), ((), ())), precision=HIGH, preferred_element_type=F32
            )

        gsrc[it] = lax.fori_loop(0, ROWS, add, jnp.zeros((T, T), F32))

    root_total = jnp.sqrt(F32(ROWS * T * 128))

    def normalised(value):
        return root_total * lax.dot_general(
            value, factor[...], (((1,), (1,)), ((), ())), precision=HIGH, preferred_element_type=F32
        )

    for it in range(ITERS):

        def forward_start():
            for d in (1, 3):
                for i in range(3):
                    gather_copy(i, d, it).wait_recv()
                    forward_copy(i, d).start()

        def second_start(d1s, d2s):
            for d2 in d2s:
                for d1 in d1s:
                    for i in range(3):
                        second_copy(i, d2, d1).start()

        if it:
            pl.semaphore_wait(free_in, len(same_core))
            for d in (1, 3):
                for i in range(3):
                    gather_copy(i, d, it).start()
        else:
            forward_start()
        for i in range(3):
            select(i, 0, it)
        second_start((0,), (1, 3, 2))
        if it:
            local_gram(0)
            gram_start(0, 0)
            lax.fori_loop(0, 5, home, 0)
            gram_finish(0, 0)
            gram_start(0, 1)
            forward_start()
        else:
            for d in STEPS:
                for i in range(3):
                    root_copy(i, d).wait_recv()
        for d in (1, 3):
            for i in range(3):
                select(i, d, it)
        second_start((1, 3), (2, 1, 3))
        if it:
            gram_finish(0, 1)
            gram_start(0, 2)
            lax.fori_loop(5, 9, home, 0)
        for i in range(3):
            for d in (1, 3):
                forward_copy(i, d).wait_recv()
            select(i, 2, it)
        second_start((2,), (2, 1, 3))
        if it:
            pl.semaphore_wait(free_out, len(all_peers))
        for i in range(3):
            third_start(i, 0)
            own_copy(i, 0).start()
        if it:
            gram_finish(0, 2)
            gram_start(0, 3)
        lax.fori_loop(9 if it else 0, ROWS, home, 0)
        for d2 in (2, 1, 3):
            for i in (1, 2, 0):
                for d1 in range(4):
                    second_copy(i, d2, d1).wait_recv()
                third_start(i, d2)
                own_copy(i, d2).start()
        if it:
            gram_finish(0, 3)
            inverse_factor(gout.at[0], factor)
        for i in range(3):
            for d in (1, 3):
                gather_copy(i, d, it).wait_send()
                forward_copy(i, d).wait_send()
            for d in STEPS:
                if it == 0:
                    root_copy(i, d).wait_send()
                for d1 in range(4):
                    second_copy(i, d, d1).wait_send()
            third_all(i).wait_send()
            for d2 in range(4):
                own_copy(i, d2).wait()
        if it == 0:
            for by in same_core:
                pl.semaphore_signal(free_in, inc=1, device_id=device(**by), device_id_type=MESH)
        for i in range(3):
            third_all(i).wait_recv()
        lax.fori_loop(0, 128 // FAR_STEP, far_products, jnp.zeros((T, T), F32))

        if it == 0:
            for by in all_peers:
                pl.semaphore_signal(free_out, inc=1, device_id=device(**by), device_id_type=MESH)

            def close(r, carry):
                image = add_far(r)
                acc[r] = image
                put(r, image * inv[r])
                return carry

            lax.fori_loop(0, ROWS, close, 0)
        else:

            def close_last(r, carry):
                acc[r] = normalised(add_far(r))
                return carry

            lax.fori_loop(0, ROWS, close_last, 0)
    local_gram(1)
    for stage in range(4):
        gram_start(1, stage)
        gram_finish(1, stage)
    inverse_factor(gout.at[1], factor)

    def finish(r, carry):
        out_ref[r] = normalised(acc[r])
        return carry

    lax.fori_loop(0, ROWS, finish, 0)


def per_device(tiles, tile_cols, tile_counts, block):
    smem, vmem = pl.BlockSpec(memory_space=pltpu.SMEM), pl.BlockSpec(memory_space=pltpu.VMEM)
    dma = pltpu.SemaphoreType.DMA
    ints = lambda *shape: jax.ShapeDtypeStruct(shape, jnp.int32)
    want, own, slot, place, keep, last = pl.pallas_call(
        index_kernel,
        out_shape=[ints(1, 128), ints(ROWS * SLOTS), ints(128), ints(3, 128), ints(128), ints(ROWS)],
        in_specs=[smem, smem],
        out_specs=[smem] * 6,
    )(tile_cols, tile_counts)
    out = pl.pallas_call(
        kernel,
        out_shape=jax.ShapeDtypeStruct((ROWS, T, T), F32),
        in_specs=[pl.BlockSpec(memory_space=pl.ANY), vmem, vmem] + [smem] * 6,
        out_specs=vmem,
        scratch_shapes=[
            pltpu.VMEM((ROWS, SLOTS, T, T), jnp.bfloat16),
            pltpu.VMEM((ROWS, SLOTS, T, T), jnp.bfloat16),
            pltpu.VMEM((128, T, T), F32),
            *[pltpu.VMEM((ROWS, n, T), F32) for n in PARTS for _ in range(3)],
            *[pltpu.VMEM((3, 4, 8, n, T), F32) for n in PARTS],
            *[pltpu.VMEM((4, 4, 8, n, T), F32) for n in PARTS],
            *[pltpu.VMEM((8, 16, n, T), F32) for n in PARTS],
            pltpu.VMEM((ROWS, T, T), F32),
            pltpu.VMEM((ROWS + 1, T, 2 * T), jnp.bfloat16),
            pltpu.VMEM((ROWS, T, T), F32),
            pltpu.VMEM((T, T), F32),
            *[pltpu.VMEM((4, n, T), F32) for n in PARTS],
            pltpu.VMEM((2, T, T), F32),
            pltpu.VMEM((2, 8, 16, T), F32),
            pltpu.VMEM((2, 2, 4, 16, T), F32),
            pltpu.VMEM((2, T, T), F32),
            pltpu.VMEM((T, T), F32),
            pltpu.VMEM((2, 4, 4, 4, 1, T), jnp.int32),
            pltpu.SMEM((2, 4, 4, 4, 1, T), jnp.int32),
            dma((ROWS,)),
            *[dma((3, 4)) for _ in range(6)],
            dma((3, 4, 4)),
            dma((3, 4, 4)),
            dma((3,)),
            dma((3,)),
            dma((3, 4)),
            dma((4, 4)),
            dma((4, 4)),
            dma,
            dma((2, 4, 8)),
            dma((2, 4, 8)),
            pltpu.SemaphoreType.REGULAR,
            pltpu.SemaphoreType.REGULAR,
        ],
        compiler_params=pltpu.CompilerParams(
            collective_id=0, has_side_effects=True, vmem_limit_bytes=63 * 2**20
        ),
    )(tiles, block.reshape(ROWS, T, T), want, own, slot, place, keep, last, tile_counts)
    return out.reshape(ROWS * T, T)


def solution(mesh):
    shard = ("row", "grp")
    return jax.shard_map(
        per_device,
        mesh=mesh,
        in_specs=(P(shard, None, None, None), P(shard, None), P(shard), P(shard, None)),
        out_specs=P(shard, None),
        check_vma=False,
    )
```

time: 280 us -> 238 us (0.85)
  Pallas kernels: 271 us -> 236 us
  other arithmetic: 3.42 us -> 0 us
    pallas_call x1, Pallas kernels: 271 us -> 226 us  [per_device(): pl.pallas_call(kernel, out_shape=jax.ShapeDtypeStruct((ROWS, T, T), F32),...]
    pallas_call x0 -> x1, Pallas kernels: none -> 9.97 us  [per_device(): pl.pallas_call(index_kernel, out_shape=[ints(1, 128), ints(ROWS * SLOTS),...]
where the time goes in v2:
time: 238 us
  Pallas kernels  236 us (99%)
    pallas_call x1, Pallas kernels, per_device(): pl.pallas_call(kernel, out_shape=jax.ShapeDtypeStruct((ROWS, T, T), F32),...  226 us
    pallas_call x1, Pallas kernels, per_device(): pl.pallas_call(index_kernel, out_shape=[ints(1, 128), ints(ROWS * SLOTS),...  9.97 us

profile of v2, /device:TPU:1, one launch (start us, length us, event | category | flops | bytes accessed | tf_op | source)
XLA Modules:
  0.0 238.0 jit_solution(7650146402338230587)
XLA Ops:
  0.0 10.0 %shard_map.46 = (s32[1,128]{1,0:T(1,128)}, s32[320]{0:T(512)}, s32[128]{0:T(128)}, s32[3,128]{1,0:T(4,128)}, s32[128]{0:T(128)}, /*index=5*/s32[16]{0:T(128)}) custom-call(s32[16,20]{1,0:T(8,128)} %cols_ref.1, s32[16]{0:T(128)} %counts_ref.3), custom_call_target="tpu_custom_call" | custom-call | tf_op jit(solution)/shard_map/pallas_call | solution.py:515
  10.0 225.8 %shard_map.47 = f32[16,128,128]{2,1,0:T(8,128)} custom-call(f32[16,20,128,128]{3,2,1,0:T(8,128)} %tiles_hbm.1, f32[16,128,128]{2,1,0:T(8,128)} %bitcast.3, s32[1,128]{1,0:T(1,128)} %get-tuple-element.11.want_ref, s32[320]{0:T(512)} %get-tuple-element.12.own_ref, s32[128]{0:T(128)} %get-tuple-element.13.slot_ref, s32[3,128]{1,0:T(4,128)} %get-tuple-element.14.place_ref, ...), custom_call_target="tpu_custom_call" | custom-call | tf_op jit(solution)/shard_map/pallas_call | solution.py:521
  235.8 2.3 copy.6

commit v3 on v2

--- a/solution.py
+++ b/solution.py
@@ -16,7 +16,7 @@
 STARTS = (0, 48, 88)
 ORDERS = (("z", "x", "y"), ("y", "z", "x"), ("x", "y", "z"))
 STEPS = (1, 3, 2)
-FAR_STEP = 8
+FAR_STEP = 16
 STAGED = 6
 HIGH = lax.Precision.HIGHEST
 F32 = jnp.float32
@@ -66,51 +66,46 @@
     lax.fori_loop(0, T // 8, block, 0)
 
 
-def index_kernel(cols_ref, counts_ref, want_ref, own_ref, slot_ref, place_ref, keep_ref, last_ref):
-    row, x = lax.axis_index("row"), lax.axis_index("grp")
-    z, y, c = row // 8, (row // 2) % 4, row % 2
-    want_ref[0, 0] = 0
-    slot_ref[127] = 0
-    keep_ref[127] = 0
-    for i in range(3):
-        place_ref[i, 127] = 0
-
-    def one_row(r, first):
-        last_ref[r] = 127
-        count = counts_ref[r]
-
-        def one_slot(s, n):
-            col = cols_ref[r, s]
-            owner, local = col >> 4, col & 15
-            away = {"x": (x - owner) & 3, "y": (y - (owner >> 3)) & 3, "z": (z - (owner >> 5)) & 3}
-            dc = (c - (owner >> 2)) & 1
-            place = away["x"] * 32 + away["y"] * 8 + away["z"] * 2 + dc
-            far = place != 0
-            k = r * SLOTS + s
-            own_ref[k] = jnp.where(far | (s >= count), ROWS, local)
-
-            @pl.when(far)
-            def _():
-                want_ref[0, place] = local
-                slot_ref[n] = k
-                for i, (a1, a2, a3) in enumerate(ORDERS):
-                    place_ref[i, n] = (away[a3] * 2 + dc) * 16 + away[a2] * 4 + away[a1]
-                keep_ref[n] = jnp.where(n == first, 0, 1)
-                last_ref[r] = n
-
-            return n + far.astype(jnp.int32)
-
-        return lax.fori_loop(0, SLOTS, one_slot, first)
-
-    lax.fori_loop(0, ROWS, one_row, jnp.int32(0))
+def index_tables(cols_ref, counts_ref, x, y, z, c):
+    sub = lax.broadcasted_iota(jnp.int32, (ROWS, T), 0)
+    lane = lax.broadcasted_iota(jnp.int32, (ROWS, T), 1)
+    counts = jnp.zeros((ROWS, T), jnp.int32)
+    for r in range(ROWS):
+        counts = jnp.where(sub == r, counts_ref[r], counts)
+    own = jnp.full((ROWS, T), ROWS, jnp.int32)
+    slots = []
+    total = jnp.zeros((ROWS, T), jnp.int32)
+    for s in range(SLOTS):
+        col = jnp.broadcast_to(cols_ref[:, s : s + 1], (ROWS, T))
+        owner, local = col >> 4, col & 15
+        away = {"x": (x - owner) & 3, "y": (y - (owner >> 3)) & 3, "z": (z - (owner >> 5)) & 3}
+        dc = (c - (owner >> 2)) & 1
+        place = away["x"] * 32 + away["y"] * 8 + away["z"] * 2 + dc
+        far = place != 0
+        own = jnp.where((lane == s) & ~far & (s < counts), local, own)
+        slots.append((far, local, place, [(away[a3] * 2 + dc) * 16 + away[a2] * 4 + away[a1] for a1, a2, a3 in ORDERS], total))
+        total = total + jnp.where(far, 1, 0)
+    before = jnp.zeros((ROWS, T), jnp.int32)
+    for r in range(ROWS - 1):
+        before = before + jnp.where(sub > r, jnp.broadcast_to(total[r : r + 1, :], (ROWS, T)), 0)
+    rows = [jnp.zeros((ROWS, T), jnp.int32) for _ in range(6)]
+    for s, (far, local, place, places, rank) in enumerate(slots):
+        hot = far & (lane == before + rank)
+        rows[0] = rows[0] + jnp.where(far & (lane == place), local, 0)
+        for n, value in enumerate([sub * SLOTS + s, *places, jnp.where(rank > 0, 1, 0)]):
+            rows[n + 1] = rows[n + 1] + jnp.where(hot, value, 0)
+    last = jnp.where(total > 0, jnp.minimum(before + total - 1, 127), 127)
+    rows.append(jnp.where(lane == sub, last, 0))
+    lists = [jnp.sum(row, axis=0, keepdims=True) for row in rows]
+    return own, lists
 
 
 def kernel(
-    tiles_hbm, block_ref, want_ref, own_ref, slot_ref, place_ref, keep_ref, last_ref, counts_ref, out_ref,
+    tiles_hbm, block_ref, cols_ref, counts_ref, out_ref,
     whi, wlo, work, ag1, ag2, ag3, ag4, ag5, ag6, ag7, ag8, ag9,
     st0, st1, st2, xr0, xr1, xr2, fn0, fn1, fn2, xs, xcat, inv, icol, ic0, ic1, ic2,
-    gsrc, gpart, gline, gout, factor, wtab, stab,
-    load_sem, s1s, s1r, fs, fr, is_, ir, s2s, s2r, s3s, s3r, loc_sem, ws, wr, tab_sem, gs, gr, free_in, free_out,
+    gsrc, gpart, gline, gout, factor, wtab, stab, own_vec, list_vec, own_ref, list_ref,
+    load_sem, s1s, s1r, fs, fr, is_, ir, s2s, s2r, s3s, s3r, loc_sem, ws, wr, tab_sem, own_sem, list_sem, gs, gr, free_in, free_out,
 ):
     ag = ((None, ag1, ag2, ag3), (None, ag4, ag5, ag6), (None, ag7, ag8, ag9))
     st, xr, fn, ic = (st0, st1, st2), (xr0, xr1, xr2), (fn0, fn1, fn2), (ic0, ic1, ic2)
@@ -134,6 +129,14 @@
     all_peers = same_core + [{a: d, "c": 1} for a in "xyz" for d in STEPS] + [{"c": 1}]
     for by in all_peers:
         pl.semaphore_signal(barrier, inc=1, device_id=device(**by), device_id_type=MESH)
+    own, lists = index_tables(cols_ref, counts_ref, at["x"], at["y"], at["z"], at["c"])
+    own_vec[...] = own
+    for n, row_list in enumerate(lists):
+        list_vec[n] = row_list
+    own_table = pltpu.make_async_copy(own_vec, own_ref, own_sem)
+    own_table.start()
+    list_table = pltpu.make_async_copy(list_vec, list_ref, list_sem)
+    list_table.start()
     pl.semaphore_wait(barrier, len(all_peers))
 
     def gather_copy(i, d, it):
@@ -158,7 +161,7 @@
             device_id=device(**{ORDERS[i][0]: d}), device_id_type=MESH,
         )
 
-    wtab[0, 0, 0, 0] = want_ref[...]
+    wtab[0, 0, 0, 0] = lists[0]
 
     def table_copies(stage):
         axis = "zyxc"[stage]
@@ -237,6 +240,8 @@
 
     lax.fori_loop(0, ROWS, begin, 0)
     table.wait()
+    own_table.wait()
+    list_table.wait()
 
     def second_copy(i, d2, d1):
         return pltpu.make_async_remote_copy(
@@ -300,7 +305,7 @@
         total = jnp.zeros((T, 2 * T), F32)
         small = jnp.zeros((T, T), F32)
         for s in range(0, SLOTS, 2):
-            b = jnp.concatenate([xcat[own_ref[r * SLOTS + s]], xcat[own_ref[r * SLOTS + s + 1]]], axis=0)
+            b = jnp.concatenate([xcat[own_ref[r, s]], xcat[own_ref[r, s + 1]]], axis=0)
             total = total + dot(jnp.concatenate([whi[r, s], whi[r, s + 1]], axis=1), b)
             small = small + dot(jnp.concatenate([wlo[r, s], wlo[r, s + 1]], axis=1), b[:, :T])
         acc[r] = total[:, :T] + (total[:, T:] + small)
@@ -310,22 +315,22 @@
         values = []
         for k in range(FAR_STEP):
             k = group * FAR_STEP + k
-            slot = slot_ref[k]
+            slot = list_ref[1, 0, k]
             pieces = []
             for i in range(3):
-                where = place_ref[i, k]
+                where = list_ref[2 + i, 0, k]
                 pieces.append(fn[i][where // 16, lax.rem(where, 16)])
             hi, lo = split(jnp.concatenate(pieces, axis=0))
             r, s = slot // SLOTS, lax.rem(slot, SLOTS)
             wide = dot(whi[r, s], jnp.concatenate([hi, lo], axis=1))
             values.append(wide[:, :T] + (wide[:, T:] + dot(wlo[r, s], hi)))
         for k in range(FAR_STEP):
-            running = jnp.where(keep_ref[group * FAR_STEP + k] > 0, running, 0.0) + values[k]
+            running = jnp.where(list_ref[5, 0, group * FAR_STEP + k] > 0, running, 0.0) + values[k]
             work[group * FAR_STEP + k] = running
         return running
 
     def add_far(r):
-        return (acc[r] + work[last_ref[r]]) * inv[r]
+        return (acc[r] + work[list_ref[6, 0, r]]) * inv[r]
 
     group = [(dx, dc) for dx in range(4) for dc in range(2) if dx or dc]
     mine = pl.multiple_of((at["x"] * 2 + at["c"]) * 16, 16)
@@ -383,7 +388,7 @@
                 a, a, (((0,), (0,)), ((), ())), precision=HIGH, preferred_element_type=F32
             )
 
-        gsrc[it] = lax.fori_loop(0, ROWS, add, jnp.zeros((T, T), F32))
+        gsrc[it] = lax.fori_loop(0, ROWS, add, jnp.zeros((T, T), F32), unroll=4)
 
     root_total = jnp.sqrt(F32(ROWS * T * 128))
 
@@ -401,10 +406,11 @@
                     forward_copy(i, d).start()
 
         def second_start(d1s, d2s):
-            for d2 in d2s:
+            for pair in d2s:
                 for d1 in d1s:
                     for i in range(3):
-                        second_copy(i, d2, d1).start()
+                        for d2 in pair:
+                            second_copy(i, d2, d1).start()
 
         if it:
             pl.semaphore_wait(free_in, len(same_core))
@@ -415,7 +421,7 @@
             forward_start()
         for i in range(3):
             select(i, 0, it)
-        second_start((0,), (1, 3, 2))
+        second_start((0,), ((2,), (1, 3)))
         if it:
             local_gram(0)
             gram_start(0, 0)
@@ -430,7 +436,7 @@
         for d in (1, 3):
             for i in range(3):
                 select(i, d, it)
-        second_start((1, 3), (2, 1, 3))
+        second_start((1, 3), ((2,), (1, 3)))
         if it:
             gram_finish(0, 1)
             gram_start(0, 2)
@@ -439,7 +445,7 @@
             for d in (1, 3):
                 forward_copy(i, d).wait_recv()
             select(i, 2, it)
-        second_start((2,), (2, 1, 3))
+        second_start((2,), ((2,), (1, 3)))
         if it:
             pl.semaphore_wait(free_out, len(all_peers))
         for i in range(3):
@@ -487,14 +493,14 @@
                 put(r, image * inv[r])
                 return carry
 
-            lax.fori_loop(0, ROWS, close, 0)
+            lax.fori_loop(0, ROWS, close, 0, unroll=2)
         else:
 
             def close_last(r, carry):
                 acc[r] = normalised(add_far(r))
                 return carry
 
-            lax.fori_loop(0, ROWS, close_last, 0)
+            lax.fori_loop(0, ROWS, close_last, 0, unroll=4)
     local_gram(1)
     for stage in range(4):
         gram_start(1, stage)
@@ -505,23 +511,16 @@
         out_ref[r] = normalised(acc[r])
         return carry
 
-    lax.fori_loop(0, ROWS, finish, 0)
+    lax.fori_loop(0, ROWS, finish, 0, unroll=4)
 
 
 def per_device(tiles, tile_cols, tile_counts, block):
     smem, vmem = pl.BlockSpec(memory_space=pltpu.SMEM), pl.BlockSpec(memory_space=pltpu.VMEM)
     dma = pltpu.SemaphoreType.DMA
-    ints = lambda *shape: jax.ShapeDtypeStruct(shape, jnp.int32)
-    want, own, slot, place, keep, last = pl.pallas_call(
-        index_kernel,
-        out_shape=[ints(1, 128), ints(ROWS * SLOTS), ints(128), ints(3, 128), ints(128), ints(ROWS)],
-        in_specs=[smem, smem],
-        out_specs=[smem] * 6,
-    )(tile_cols, tile_counts)
     out = pl.pallas_call(
         kernel,
         out_shape=jax.ShapeDtypeStruct((ROWS, T, T), F32),
-        in_specs=[pl.BlockSpec(memory_space=pl.ANY), vmem, vmem] + [smem] * 6,
+        in_specs=[pl.BlockSpec(memory_space=pl.ANY), vmem, vmem, smem],
         out_specs=vmem,
         scratch_shapes=[
             pltpu.VMEM((ROWS, SLOTS, T, T), jnp.bfloat16),
@@ -543,6 +542,10 @@
             pltpu.VMEM((T, T), F32),
             pltpu.VMEM((2, 4, 4, 4, 1, T), jnp.int32),
             pltpu.SMEM((2, 4, 4, 4, 1, T), jnp.int32),
+            pltpu.VMEM((ROWS, T), jnp.int32),
+            pltpu.VMEM((7, 1, T), jnp.int32),
+            pltpu.SMEM((ROWS, T), jnp.int32),
+            pltpu.SMEM((7, 1, T), jnp.int32),
             dma((ROWS,)),
             *[dma((3, 4)) for _ in range(6)],
             dma((3, 4, 4)),
@@ -553,6 +556,8 @@
             dma((4, 4)),
             dma((4, 4)),
             dma,
+            dma,
+            dma,
             dma((2, 4, 8)),
             dma((2, 4, 8)),
             pltpu.SemaphoreType.REGULAR,
@@ -561,7 +566,7 @@
         compiler_params=pltpu.CompilerParams(
             collective_id=0, has_side_effects=True, vmem_limit_bytes=63 * 2**20
         ),
-    )(tiles, block.reshape(ROWS, T, T), want, own, slot, place, keep, last, tile_counts)
+    )(tiles, block.reshape(ROWS, T, T), tile_cols, tile_counts)
     return out.reshape(ROWS * T, T)
 
 

time: 238 us -> 221 us (0.929)
  Pallas kernels: 236 us -> 219 us
    pallas_call x1 -> x0, Pallas kernels: 9.97 us -> none  [per_device(): pl.pallas_call(index_kernel, out_shape=[ints(1, 128), ints(ROWS * SLOTS),...]
    pallas_call x1, Pallas kernels: 226 us -> 219 us  [per_device(): pl.pallas_call(kernel, out_shape=jax.ShapeDtypeStruct((ROWS, T, T), F32),...]
where the time goes in v3:
time: 221 us
  Pallas kernels  219 us (99%)
  local copies, waits for them, and re-layouts  2.26 us (1%)
    pallas_call x1, Pallas kernels, per_device(): pl.pallas_call(kernel, out_shape=jax.ShapeDtypeStruct((ROWS, T, T), F32),...  219 us

profile of v3, /device:TPU:1, one launch (start us, length us, event | category | flops | bytes accessed | tf_op | source)
XLA Modules:
  0.0 220.9 jit_solution(17709464547173529812)
XLA Ops:
  0.0 218.6 %shard_map.46 = f32[16,128,128]{2,1,0:T(8,128)} custom-call(f32[16,20,128,128]{3,2,1,0:T(8,128)} %tiles_hbm.1, f32[16,128,128]{2,1,0:T(8,128)} %bitcast.3, s32[16,20]{1,0:T(8,128)} %cols_ref.1, s32[16]{0:T(128)} %counts_ref.1), custom_call_target="tpu_custom_call" | custom-call | tf_op jit(solution)/shard_map/pallas_call | solution.py:520
  218.6 2.3 %copy.6 = f32[2048,128]{1,0:T(8,128)} copy(f32[2048,128]{1,0:T(8,128)} %bitcast.2) | data formatting | bytes 2097152

commit v4 on v3

--- a/solution.py
+++ b/solution.py
@@ -194,7 +194,7 @@
             wlo[r, s] = lo
             return total + tile * jnp.where(s < count, 1.0, 0.0)
 
-        total = lax.fori_loop(0, SLOTS, add, jnp.zeros((T, T), F32), unroll=4)
+        total = lax.fori_loop(0, SLOTS, add, jnp.zeros((T, T), F32), unroll=8)
         root = 1.0 / jnp.sqrt(jnp.sum(total, axis=1, keepdims=True))
         inv[r] = jnp.broadcast_to(root, (T, T))
         return jnp.where(lane == r, root, columns)
@@ -272,7 +272,7 @@
                     st[i][d2 - 1, d1, e] = value
                 return carry
 
-            lax.fori_loop(0, 8, pick, 0, unroll=4)
+            lax.fori_loop(0, 8, pick, 0, unroll=8)
 
     def third_start(i, d2):
         a3 = ORDERS[i][2]
@@ -388,7 +388,7 @@
                 a, a, (((0,), (0,)), ((), ())), precision=HIGH, preferred_element_type=F32
             )
 
-        gsrc[it] = lax.fori_loop(0, ROWS, add, jnp.zeros((T, T), F32), unroll=4)
+        gsrc[it] = lax.fori_loop(0, ROWS, add, jnp.zeros((T, T), F32), unroll=8)
 
     root_total = jnp.sqrt(F32(ROWS * T * 128))
 
@@ -493,14 +493,14 @@
                 put(r, image * inv[r])
                 return carry
 
-            lax.fori_loop(0, ROWS, close, 0, unroll=2)
+            lax.fori_loop(0, ROWS, close, 0, unroll=4)
         else:
 
             def close_last(r, carry):
                 acc[r] = normalised(add_far(r))
                 return carry
 
-            lax.fori_loop(0, ROWS, close_last, 0, unroll=4)
+            lax.fori_loop(0, ROWS, close_last, 0, unroll=8)
     local_gram(1)
     for stage in range(4):
         gram_start(1, stage)
@@ -511,7 +511,7 @@
         out_ref[r] = normalised(acc[r])
         return carry
 
-    lax.fori_loop(0, ROWS, finish, 0, unroll=4)
+    lax.fori_loop(0, ROWS, finish, 0, unroll=8)
 
 
 def per_device(tiles, tile_cols, tile_counts, block):

time: 221 us -> 220 us (level)
  no operation moved by 1% of the time
where the time goes in v4:
time: 220 us
  Pallas kernels  218 us (99%)
  local copies, waits for them, and re-layouts  2.26 us (1%)
    pallas_call x1, Pallas kernels, per_device(): pl.pallas_call(kernel, out_shape=jax.ShapeDtypeStruct((ROWS, T, T), F32),...  218 us

profile of v4, /device:TPU:1, one launch (start us, length us, event | category | flops | bytes accessed | tf_op | source)
XLA Modules:
  0.0 220.0 jit_solution(14927715397858355326)
XLA Ops:
  0.0 217.7 %shard_map.46 = f32[16,128,128]{2,1,0:T(8,128)} custom-call(f32[16,20,128,128]{3,2,1,0:T(8,128)} %tiles_hbm.1, f32[16,128,128]{2,1,0:T(8,128)} %bitcast.3, s32[16,20]{1,0:T(8,128)} %cols_ref.1, s32[16]{0:T(128)} %counts_ref.1), custom_call_target="tpu_custom_call" | custom-call | tf_op jit(solution)/shard_map/pallas_call | solution.py:520
  217.7 2.3 %copy.6 = f32[2048,128]{1,0:T(8,128)} copy(f32[2048,128]{1,0:T(8,128)} %bitcast.2) | data formatting | bytes 2097152
